TPU v7x, 32 devices: a whole 2x2x4 slice. The times are simulated.
32 devices in a mesh: pipe: 4 (over x, core), dp: 2 (over y), vocab: 4 (over z).
Axes of the slice: x: 2, y: 2, z: 4, core: 2. Of those that a mesh axis runs over, the one named last changes fastest.
Arguments:
- hidden: bfloat16 [512, 4608], P(('pipe', 'dp', 'vocab')), may hold values from -6 to 6
- targets: int32 [512], P(('pipe', 'dp', 'vocab')), may hold values from 0 to 12287, as said below
- input_ids: int32 [512], P(('pipe', 'dp', 'vocab')), may hold values from 0 to 12287, as said below
- input_grads: bfloat16 [512, 4608], P(('pipe', 'dp', 'vocab')), may hold values from -0.3125 to 0.3125
- table: bfloat16 [12288, 4608], P(('pipe', 'vocab'), 'dp'), may hold values from -0.75 to 0.75
- keep: int32 [12288], P(('pipe', 'vocab')), may hold values from 0 to 1
- first_moment: bfloat16 [12288, 4608], P(('pipe', 'vocab'), 'dp'), may hold values from -0.015625 to 0.015625
- second_moment: bfloat16 [12288, 4608], P(('pipe', 'vocab'), 'dp'), may hold values from 9.983778e-07 to 9.953976e-06
Outputs:
- new_table: bfloat16 [12288, 4608], P(('pipe', 'vocab'), 'dp')
- new_first: bfloat16 [12288, 4608], P(('pipe', 'vocab'), 'dp')
- new_second: bfloat16 [12288, 4608], P(('pipe', 'vocab'), 'dp')
- loss: float32 [], replicated
Inputs may be any that keep to these rules, and one draw needn't show every extreme that they name: `targets`: names only rows with keep = 1. `input_ids`: names only rows with keep = 1.
All inputs are finite; a program needn't handle non-finite values.
Results may differ from a plain program's by a relative error of at most 0.0036.
Values may be sent and summed in bfloat16 or wider, within the bound.
A program may use at most 192 MiB of HBM per device.

v0:
```python
import math
import jax
import jax.numpy as jnp
from jax import lax
from jax.sharding import PartitionSpec as P

SOFTCAP = 30.0
LEARN = 0.01
EPSILON = 1e-08


def contract_last(left, right):
    return lax.dot_general(
        left, right, (((1,), (1,)), ((), ())), preferred_element_type=jnp.float32
    )


def contract_first(left, right):
    return lax.dot_general(
        left, right, (((0,), (0,)), ((), ())), preferred_element_type=jnp.float32
    )


def body(hidden, targets, input_ids, input_grads, table, keep, first_moment, second_moment):
    rows_here = table.shape[0]
    row_start = lax.axis_index(("pipe", "vocab")) * rows_here
    keepf = keep.astype(jnp.float32)
    scale = math.sqrt(hidden.shape[1])
    groups_dp = lax.axis_size("dp")
    row_iota = jnp.arange(rows_here, dtype=jnp.int32)
    both = jnp.stack([targets, input_ids])
    packed = lax.all_to_all(
        jnp.stack([hidden, input_grads]), "dp", split_axis=2, concat_axis=1, tiled=True
    )
    ids_all = lax.all_gather(both, ("pipe", "vocab", "dp"), axis=1, tiled=True)
    tokens_all = lax.all_gather(packed[0], ("pipe", "vocab"), axis=0, tiled=True)
    grads_all = lax.all_gather(packed[1], ("pipe", "vocab"), axis=0, tiled=True)
    tokens = tokens_all.shape[0]
    share = tokens // groups_dp
    start = lax.axis_index("dp") * share
    goals = lax.dynamic_slice(ids_all[0], (start,), (share,))
    raw = lax.psum_scatter(contract_last(tokens_all, table), "dp", scatter_dimension=0, tiled=True)
    capped = SOFTCAP * jnp.tanh(raw / SOFTCAP)
    onehot = ((goals - row_start)[:, None] == row_iota[None, :]).astype(jnp.float32)
    weights = jnp.exp(capped) * keepf[None, :]
    local = jnp.stack([jnp.sum(weights, axis=1), jnp.sum(capped * onehot, axis=1)])
    placed = lax.dynamic_update_slice(jnp.zeros((2, tokens), jnp.float32), local, (0, start))
    sums = lax.psum(placed, ("pipe", "dp", "vocab"))
    token_loss = jnp.sum(jnp.log(sums[0]) - sums[1])
    total = lax.dynamic_slice(sums[0], (start,), (share,))
    slope = 1.0 - (capped / SOFTCAP) ** 2
    dlogits = ((weights / total[:, None] - onehot) * slope).astype(jnp.bfloat16)
    dlogits = lax.all_gather(dlogits, "dp", axis=0, tiled=True)
    selector = ((ids_all[1] - row_start)[None, :] == row_iota[:, None]).astype(jnp.bfloat16)
    finished = contract_first(dlogits, tokens_all) + scale * jnp.dot(
        selector, grads_all, preferred_element_type=jnp.float32
    )
    kept = keep[:, None] > 0
    first_new = (0.9 * first_moment.astype(jnp.float32) + 0.1 * finished).astype(jnp.bfloat16)
    second_new = (0.95 * second_moment.astype(jnp.float32) + 0.05 * finished * finished).astype(
        jnp.bfloat16
    )
    corr_one = 1.0 - 0.9**10
    corr_two = 1.0 - 0.95**10
    update = (
        first_new.astype(jnp.float32)
        / corr_one
        / (jnp.sqrt(second_new.astype(jnp.float32) / corr_two) + EPSILON)
    )
    table_new = (table.astype(jnp.float32) - LEARN * update).astype(jnp.bfloat16)
    new_table = jnp.where(kept, table_new, table)
    new_first = jnp.where(kept, first_new, first_moment)
    new_second = jnp.where(kept, second_new, second_moment)
    return (new_table, new_first, new_second, token_loss)


def solution(mesh):
    placed = (
        P(("pipe", "dp", "vocab"), None),
        P(("pipe", "dp", "vocab")),
        P(("pipe", "dp", "vocab")),
        P(("pipe", "dp", "vocab"), None),
        P(("pipe", "vocab"), "dp"),
        P(("pipe", "vocab")),
        P(("pipe", "vocab"), "dp"),
        P(("pipe", "vocab"), "dp"),
    )
    return jax.shard_map(
        body,
        mesh=mesh,
        in_specs=placed,
        out_specs=(
            P(("pipe", "vocab"), "dp"),
            P(("pipe", "vocab"), "dp"),
            P(("pipe", "vocab"), "dp"),
            P(),
        ),
        check_vma=False,
    )
```

profile of v0, /device:TPU:10, one launch (start us, length us, event | category | flops | bytes accessed | tf_op | source)
XLA Modules:
  0.0 227.2 jit_solution(489731304706484116)
XLA Ops:
  7.2 0.0 all-gather.4.cloned.1.call-start
  7.2 1.0 pad_maximum_fusion
  8.2 3.0 %copy.27 = bf16[2,16,4608]{1,0,2:T(2,128)(2,1)S(1)} copy(bf16[2,16,4608]{2,1,0:T(8,128)(2,1)S(1)} %pad_maximum_fusion) | data formatting | bytes 589824 | tf_op jit(solution)/shard_map/stack | solution.py:33
  11.2 2.5 %reshape.30 = bf16[2,2,36864]{2,1,0:T(2,128)(2,1)S(1)} reshape(bf16[4608,2,16]{2,1,0:T(2,128)(2,1)S(1)} %bitcast.27) | data formatting | bytes 589824
  13.7 8.2 %all_to_all.15 = bf16[2,2,36864]{2,1,0:T(2,128)(2,1)S(1)} all-to-all(bf16[2,2,36864]{2,1,0:T(2,128)(2,1)S(1)} %reshape.30), channel_id=1, replica_groups=mesh['pipe'=4,'dp'=2,'vocab'=4] {'dp'}, dimensions={0} | all-to-all | bytes 589824 | tf_op jit(solution)/shard_map/all_to_all | solution.py:32
  21.9 1.6 reshape.31
  23.5 1.6 copy.32
  25.1 0.2 fusion.6
  25.3 0.7 copy.29
  26.0 0.0 all-gather.4.cloned.1.call-update
  26.0 0.0 copy-start.1
  26.0 0.0 copy-start.2
  26.0 0.0 copy-start.3
  26.1 0.0 reduce-scatter.2.cloned.1.call-start
  26.1 41.0 %all-gather.4.cloned.1.call-done = bf16[512,2304]{1,0:T(8,128)(2,1)} async-done(((bf16[32,2304]{1,0:T(8,128)(2,1)}), bf16[512,2304]{1,0:T(8,128)(2,1)}) %all-gather.4.cloned.1.call-update) | async-done | bytes 2359312 | tf_op jit(solution)/shard_map/all_gather | solution.py:36
  67.2 5.9 %fusion.7 = f32[512,768]{1,0:T(8,128)} fusion(bf16[512,2304]{1,0:T(8,128)(2,1)} %all-gather.4.cloned.1.call-done, bf16[768,2304]{1,0:T(8,128)(2,1)} %param.12), kind=kOutput, calls=%fused_computation.27 | convolution fusion | flops 1811939328 | bytes 7471104 | tf_op jit(solution)/shard_map/dot_general | solution.py:13
  73.0 0.0 copy-start
  73.0 0.0 reduce-scatter.2.cloned.1.call-update
  73.1 0.0 all-gather.6.cloned.1.call-start
  73.1 0.7 copy.31
  73.8 0.0 all-gather.6.cloned.1.call-update
  73.8 0.0 copy-done.1
  73.8 0.0 copy-done.2
  73.9 0.0 copy-done.3
  73.9 65.0 %all-gather = s32[32,16,2]{1,2,0:T(2,128)S(1)} all-gather(s32[1,16,2]{1,2,0:T(2,128)S(1)} %add_bitcast_fusion), channel_id=1, replica_groups=mesh['pipe'=4,'dp'=2,'vocab'=4] {'pipe','vocab','dp'}, dimensions={0}, use_global_device_ids=true | all-gather | bytes 4224 | tf_op jit(solution)/shard_map/all_gather | solution.py:35
  138.8 0.1 reshape.29
  139.0 0.0 reduce-scatter.2.cloned.1.call-done
  139.0 1.6 fusion.4
  140.7 42.0 %psum.7 = f32[2,512]{1,0:T(2,128)S(1)} all-reduce(f32[2,512]{1,0:T(2,128)S(1)} %maximum_dynamic-update-slice_fusion), channel_id=1, replica_groups=mesh['pipe'=4,'dp'=2,'vocab'=4] {'pipe','dp','vocab'}, use_global_device_ids=true, to_apply=%region_3.0 | all-reduce | flops 1024 | bytes 8192 | tf_op jit(solution)/shard_map/psum | solution.py:48
  182.6 0.6 fusion.5
  183.2 1.5 multiply_convert_fusion
  184.8 10.6 %all_gather.14 = bf16[512,768]{1,0:T(8,128)(2,1)S(1)} all-gather(bf16[256,768]{1,0:T(8,128)(2,1)S(1)} %multiply_convert_fusion), channel_id=1, replica_groups=mesh['pipe'=4,'dp'=2,'vocab'=4] {'dp'}, dimensions={0}, use_global_device_ids=true | all-gather | bytes 1179648 | tf_op jit(solution)/shard_map/all_gather | solution.py:53
  195.4 0.0 copy-done
  195.4 5.0 %fusion.8 = f32[768,2304]{1,0:T(8,128)} fusion(bf16[512,768]{1,0:T(8,128)(2,1)S(1)} %all_gather.14, bf16[512,2304]{1,0:T(8,128)(2,1)S(1)} %copy-done), kind=kOutput, calls=%fused_computation.28 | convolution fusion | flops 1811939328 | bytes 10223616 | tf_op jit(solution)/shard_map/dot_general | solution.py:19
  200.4 0.0 all-gather.6.cloned.1.call-done
  200.4 20.3 %broadcast_select_fusion = (bf16[768,2304]{1,0:T(8,128)(2,1)}, bf16[768,2304]{1,0:T(8,128)(2,1)}, bf16[768,2304]{1,0:T(8,128)(2,1)}) fusion(bf16[768,2304]{1,0:T(8,128)(2,1)} %param.15, pred[768]{0:T(1024)(128)(4,1)S(1)} %broadcast_compare_fusion, bf16[768,2304]{1,0:T(8,128)(2,1)} %param.12, bf16[768,2304]{1,0:T(8,128)(2,1)} %param.14, ...), kind=kOutput, calls=%fused_computation.7 | convolution fusion | flops 1858338816 | bytes 30673664 | tf_op jit(solution)/shard_map/dot_general | solution.py:55
  (9 shorter events, 0.1 us)
Async XLA Ops:
  7.2 60.0 %all-gather.4.cloned.1.call-start = ((), (), s32[]{:S(2)}) async-start(), calls=%async_computation.2 | async-start | bytes 2506752 | tf_op jit(solution)/shard_map/all_gather | solution.py:36
  26.0 47.8 %copy-start.1 = (s32[768]{0:T(1024)S(1)}, s32[768]{0:T(1024)}, u32[]{:S(2)}) copy-start(s32[768]{0:T(1024)} %param.13) | copy-start | bytes 9220
  26.0 47.8 %copy-start.2 = (s32[16]{0:T(128)S(1)}, s32[16]{0:T(128)}, u32[]{:S(2)}) copy-start(s32[16]{0:T(128)} %param.10) | copy-start | bytes 196
  26.0 47.8 %copy-start.3 = (s32[16]{0:T(128)S(1)}, s32[16]{0:T(128)}, u32[]{:S(2)}) copy-start(s32[16]{0:T(128)} %param.9) | copy-start | bytes 196
  26.1 113.0 %reduce-scatter.2.cloned.1.call-start = ((), (), s32[]{:S(2)}) async-start(), calls=%async_computation.3 | async-start | bytes 2359296 | tf_op jit(solution)/shard_map/reduce_scatter | solution.py:42
  73.0 122.4 %copy-start = (bf16[512,2304]{1,0:T(8,128)(2,1)S(1)}, bf16[512,2304]{1,0:T(8,128)(2,1)}, u32[]{:S(2)}) copy-start(bf16[512,2304]{1,0:T(8,128)(2,1)} %all-gather.4.cloned.1.call-done) | copy-start | bytes 7077892
  73.1 127.3 %all-gather.6.cloned.1.call-start = ((), (), s32[]{:S(2)}) async-start(), calls=%async_computation.4 | async-start | bytes 2506752 | tf_op jit(solution)/shard_map/all_gather | solution.py:37
Sparse Core Ops, SparseCore 0:
  26.1 40.9 all-gather.3
  73.2 26.5 reduce-scatter.1
  102.9 40.8 all-gather.5
where the time goes:
time: 228 us; the launch traced here: 227 us
  blocking collectives  126 us (55%)
  waiting for transfers between devices  41.1 us (18%)
  matrix products  31.1 us (14%)
  between operations  13.9 us (6%)
  local copies, waits for them, and re-layouts  10.4 us (5%)
  other arithmetic  4.81 us (2%)
    all_gather x1, blocking collectives, body(): ids_all = lax.all_gather(both, ('pipe', 'vocab', 'dp'), axis=1, tiled=True)  65 us
    psum x1, blocking collectives, body(): sums = lax.psum(placed, ('pipe', 'dp', 'vocab'))  42 us
    all_gather x1, waiting for transfers between devices, body(): lax.all_gather(packed[0], ('pipe', 'vocab'), axis=0, tiled=True)  41 us
    dot_general x1, matrix products, body(): jnp.dot(selector, grads_all, preferred_element_type=jnp.float32)  20.3 us
    all_gather x1, blocking collectives, body(): dlogits = lax.all_gather(dlogits, 'dp', axis=0, tiled=True)  10.6 us
    all_to_all x1, blocking collectives, body(): lax.all_to_all(jnp.stack([hidden, input_grads]), 'dp', split_axis=2, conc...  8.17 us
    dot_general x1, matrix products, contract_last(): lax.dot_general(left, right, (((1,), (1,)), ((), ())), preferred_element_...  5.88 us
    dot_general x1, matrix products, contract_first(): lax.dot_general(left, right, (((0,), (0,)), ((), ())), preferred_element_...  4.95 us
  transfers between devices with their start and end apart: 3, of which 1 were waited for; matrix products, arithmetic and copies ran while one was open for 4% of the time, Pallas kernels for 0%

commit v1 on v0

--- a/solution.py
+++ b/solution.py
@@ -7,6 +7,9 @@
 SOFTCAP = 30.0
 LEARN = 0.01
 EPSILON = 1e-08
+_define_meshes = lambda s0, axis_tag, link_axis: jax.lax.psum(
+    jax.lax.psum(s0, axis_name=axis_tag), axis_name=link_axis
+)
 
 
 def contract_last(left, right):
@@ -45,7 +48,7 @@
     weights = jnp.exp(capped) * keepf[None, :]
     local = jnp.stack([jnp.sum(weights, axis=1), jnp.sum(capped * onehot, axis=1)])
     placed = lax.dynamic_update_slice(jnp.zeros((2, tokens), jnp.float32), local, (0, start))
-    sums = lax.psum(placed, ("pipe", "dp", "vocab"))
+    sums = _define_meshes(placed, ("dp", "vocab"), "pipe")
     token_loss = jnp.sum(jnp.log(sums[0]) - sums[1])
     total = lax.dynamic_slice(sums[0], (start,), (share,))
     slope = 1.0 - (capped / SOFTCAP) ** 2

time: 228 us -> 214 us (0.939)
  blocking collectives: 126 us -> 111 us
    psum x1 -> x2, blocking collectives: 42 us -> 26.1 us  [the longest x1 20.5 us: jax.lax.psum(s0, axis_name=axis_tag)]
where the time goes in v1:
time: 214 us; the launch traced here: 212 us
  blocking collectives  111 us (52%)
  waiting for transfers between devices  41.1 us (19%)
  matrix products  31.1 us (15%)
  between operations  13.9 us (6%)
  local copies, waits for them, and re-layouts  10.4 us (5%)
  other arithmetic  4.82 us (2%)
    all_gather x1, blocking collectives, body(): ids_all = lax.all_gather(both, ('pipe', 'vocab', 'dp'), axis=1, tiled=True)  65 us
    all_gather x1, waiting for transfers between devices, body(): lax.all_gather(packed[0], ('pipe', 'vocab'), axis=0, tiled=True)  41 us
    psum x1, blocking collectives, jax.lax.psum(s0, axis_name=axis_tag)  20.5 us
    dot_general x1, matrix products, body(): jnp.dot(selector, grads_all, preferred_element_type=jnp.float32)  20.3 us
    all_gather x1, blocking collectives, body(): dlogits = lax.all_gather(dlogits, 'dp', axis=0, tiled=True)  11.6 us
    all_to_all x1, blocking collectives, body(): lax.all_to_all(jnp.stack([hidden, input_grads]), 'dp', split_axis=2, conc...  8.17 us
    dot_general x1, matrix products, contract_last(): lax.dot_general(left, right, (((1,), (1,)), ((), ())), preferred_element_...  5.88 us
    psum x1, blocking collectives, jax.lax.psum(jax.lax.psum(s0, axis_name=axis_tag), axis_name=link_axis)  5.67 us
  transfers between devices with their start and end apart: 3, of which 1 were waited for; matrix products, arithmetic and copies ran while one was open for 4% of the time, Pallas kernels for 0%

profile of v1, /device:TPU:10, one launch (start us, length us, event | category | flops | bytes accessed | tf_op | source)
XLA Modules:
  0.0 212.3 jit_solution(16045910925544246098)
XLA Ops:
  7.2 0.0 all-gather.4.cloned.1.call-start
  7.2 1.0 pad_maximum_fusion
  8.2 3.0 %copy.27 = bf16[2,16,4608]{1,0,2:T(2,128)(2,1)S(1)} copy(bf16[2,16,4608]{2,1,0:T(8,128)(2,1)S(1)} %pad_maximum_fusion) | data formatting | bytes 589824 | tf_op jit(solution)/shard_map/stack | solution.py:36
  11.2 2.5 %reshape.30 = bf16[2,2,36864]{2,1,0:T(2,128)(2,1)S(1)} reshape(bf16[4608,2,16]{2,1,0:T(2,128)(2,1)S(1)} %bitcast.27) | data formatting | bytes 589824
  13.7 8.2 %all_to_all.15 = bf16[2,2,36864]{2,1,0:T(2,128)(2,1)S(1)} all-to-all(bf16[2,2,36864]{2,1,0:T(2,128)(2,1)S(1)} %reshape.30), channel_id=1, replica_groups=mesh['pipe'=4,'dp'=2,'vocab'=4] {'dp'}, dimensions={0} | all-to-all | bytes 589824 | tf_op jit(solution)/shard_map/all_to_all | solution.py:35
  21.9 1.6 reshape.31
  23.5 1.6 copy.32
  25.1 0.2 fusion.6
  25.3 0.7 copy.29
  26.0 0.0 all-gather.4.cloned.1.call-update
  26.0 0.0 copy-start.1
  26.0 0.0 copy-start.2
  26.0 0.0 copy-start.3
  26.1 0.0 reduce-scatter.2.cloned.1.call-start
  26.1 41.0 %all-gather.4.cloned.1.call-done = bf16[512,2304]{1,0:T(8,128)(2,1)} async-done(((bf16[32,2304]{1,0:T(8,128)(2,1)}), bf16[512,2304]{1,0:T(8,128)(2,1)}) %all-gather.4.cloned.1.call-update) | async-done | bytes 2359312 | tf_op jit(solution)/shard_map/all_gather | solution.py:39
  67.2 5.9 %fusion.7 = f32[512,768]{1,0:T(8,128)} fusion(bf16[512,2304]{1,0:T(8,128)(2,1)} %all-gather.4.cloned.1.call-done, bf16[768,2304]{1,0:T(8,128)(2,1)} %param.12), kind=kOutput, calls=%fused_computation.27 | convolution fusion | flops 1811939328 | bytes 7471104 | tf_op jit(solution)/shard_map/dot_general | solution.py:16
  73.0 0.0 copy-start
  73.0 0.0 reduce-scatter.2.cloned.1.call-update
  73.1 0.0 all-gather.6.cloned.1.call-start
  73.1 0.7 copy.31
  73.8 0.0 all-gather.6.cloned.1.call-update
  73.8 0.0 copy-done.1
  73.8 0.0 copy-done.2
  73.9 0.0 copy-done.3
  73.9 65.0 %all-gather = s32[32,16,2]{1,2,0:T(2,128)S(1)} all-gather(s32[1,16,2]{1,2,0:T(2,128)S(1)} %add_bitcast_fusion), channel_id=1, replica_groups=mesh['pipe'=4,'dp'=2,'vocab'=4] {'pipe','vocab','dp'}, dimensions={0}, use_global_device_ids=true | all-gather | bytes 4224 | tf_op jit(solution)/shard_map/all_gather | solution.py:38
  138.8 0.1 reshape.29
  139.0 0.0 reduce-scatter.2.cloned.1.call-done
  139.0 1.6 fusion.4
  140.7 20.5 %psum.14 = f32[2,512]{1,0:T(2,128)S(1)} all-reduce(f32[2,512]{1,0:T(2,128)S(1)} %maximum_dynamic-update-slice_fusion), channel_id=1, replica_groups=mesh['pipe'=4,'dp'=2,'vocab'=4] {'dp','vocab'}, use_global_device_ids=true, to_apply=%region_3.0 | all-reduce | flops 1024 | bytes 8192 | tf_op jit(solution)/shard_map/psum | solution.py:11
  161.1 5.7 %psum.15 = f32[2,512]{1,0:T(2,128)S(1)} all-reduce(f32[2,512]{1,0:T(2,128)S(1)} %psum.14), channel_id=1, replica_groups=mesh['pipe'=4,'dp'=2,'vocab'=4] {'pipe'}, use_global_device_ids=true, to_apply=%region_4.0 | all-reduce | flops 1024 | bytes 8192 | tf_op jit(solution)/shard_map/psum | solution.py:10
  166.8 0.6 fusion.5
  167.4 1.5 multiply_convert_fusion
  169.0 11.6 %all_gather.14 = bf16[512,768]{1,0:T(8,128)(2,1)S(1)} all-gather(bf16[256,768]{1,0:T(8,128)(2,1)S(1)} %multiply_convert_fusion), channel_id=1, replica_groups=mesh['pipe'=4,'dp'=2,'vocab'=4] {'dp'}, dimensions={0}, use_global_device_ids=true | all-gather | bytes 1179648 | tf_op jit(solution)/shard_map/all_gather | solution.py:56
  180.5 0.0 copy-done
  180.5 4.9 %fusion.8 = f32[768,2304]{1,0:T(8,128)} fusion(bf16[512,768]{1,0:T(8,128)(2,1)S(1)} %all_gather.14, bf16[512,2304]{1,0:T(8,128)(2,1)S(1)} %copy-done), kind=kOutput, calls=%fused_computation.28 | convolution fusion | flops 1811939328 | bytes 10223616 | tf_op jit(solution)/shard_map/dot_general | solution.py:22
  185.5 0.0 all-gather.6.cloned.1.call-done
  185.5 20.3 %broadcast_select_fusion = (bf16[768,2304]{1,0:T(8,128)(2,1)}, bf16[768,2304]{1,0:T(8,128)(2,1)}, bf16[768,2304]{1,0:T(8,128)(2,1)}) fusion(bf16[768,2304]{1,0:T(8,128)(2,1)} %param.15, pred[768]{0:T(1024)(128)(4,1)S(1)} %broadcast_compare_fusion, bf16[768,2304]{1,0:T(8,128)(2,1)} %param.12, bf16[768,2304]{1,0:T(8,128)(2,1)} %param.14, ...), kind=kOutput, calls=%fused_computation.7 | convolution fusion | flops 1858338816 | bytes 30673664 | tf_op jit(solution)/shard_map/dot_general | solution.py:58
  (9 shorter events, 0.1 us)
Async XLA Ops:
  7.2 60.0 %all-gather.4.cloned.1.call-start = ((), (), s32[]{:S(2)}) async-start(), calls=%async_computation.2 | async-start | bytes 2506752 | tf_op jit(solution)/shard_map/all_gather | solution.py:39
  26.0 47.8 %copy-start.1 = (s32[768]{0:T(1024)S(1)}, s32[768]{0:T(1024)}, u32[]{:S(2)}) copy-start(s32[768]{0:T(1024)} %param.13) | copy-start | bytes 9220
  26.0 47.8 %copy-start.2 = (s32[16]{0:T(128)S(1)}, s32[16]{0:T(128)}, u32[]{:S(2)}) copy-start(s32[16]{0:T(128)} %param.10) | copy-start | bytes 196
  26.0 47.8 %copy-start.3 = (s32[16]{0:T(128)S(1)}, s32[16]{0:T(128)}, u32[]{:S(2)}) copy-start(s32[16]{0:T(128)} %param.9) | copy-start | bytes 196
  26.1 113.0 %reduce-scatter.2.cloned.1.call-start = ((), (), s32[]{:S(2)}) async-start(), calls=%async_computation.3 | async-start | bytes 2359296 | tf_op jit(solution)/shard_map/reduce_scatter | solution.py:45
  73.0 107.5 %copy-start = (bf16[512,2304]{1,0:T(8,128)(2,1)S(1)}, bf16[512,2304]{1,0:T(8,128)(2,1)}, u32[]{:S(2)}) copy-start(bf16[512,2304]{1,0:T(8,128)(2,1)} %all-gather.4.cloned.1.call-done) | copy-start | bytes 7077892
  73.1 112.4 %all-gather.6.cloned.1.call-start = ((), (), s32[]{:S(2)}) async-start(), calls=%async_computation.4 | async-start | bytes 2506752 | tf_op jit(solution)/shard_map/all_gather | solution.py:40
Sparse Core Ops, SparseCore 0:
  26.1 40.9 all-gather.3
  73.2 26.5 reduce-scatter.1
  102.9 40.9 all-gather.5
